TPU v7x, 128 devices: a whole 4x4x4 slice. The times are simulated.
128 devices in a mesh: bin: 4 (over x_hi, core), slab: 32 (over z, x_lo, y).
Axes of the slice: x: 4 (x_hi: 2, x_lo: 2; x = x_hi * 2 + x_lo), y: 4, z: 4, core: 2. Of those that a mesh axis runs over, the one named last changes fastest.
Arguments:
- volumes: float32 [8, 128, 256, 512], P('bin', 'slab'), may hold values from -6 to 6
- attenuation: float32 [8, 3], replicated, may hold values from 0.2 to 1.2
- penalty: float32 [1], replicated, may hold values from 0.2 to 0.4
- tv_weight: float32 [1], replicated, may hold values from 0.3 to 0.8
Outputs:
- materials: float32 [3, 128, 256, 512], P(None, ('bin', 'slab'))
All inputs are finite; a program needn't handle non-finite values.
Results may differ from a plain program's by a relative error of at most 0.0001.
Values sent between devices are 32-bit elements; how exact they have to be, the bound alone decides.
A program may use at most 64 MiB of HBM per device.

v0:
```python
import jax
import jax.numpy as jnp
from jax import lax
from jax.experimental import pallas as pl
from jax.experimental.pallas import tpu as pltpu
from jax.sharding import PartitionSpec as P

MESH = pl.DeviceIdType.MESH
F32 = jnp.float32
HALO = 3
LAYERS = 16 + 2 * HALO
NX = 512


def position():
    bin_index = lax.axis_index("bin")
    slab_index = lax.axis_index("slab")
    return (
        bin_index // 2,
        bin_index % 2,
        slab_index // 16,
        (slab_index // 8) % 2,
        (slab_index // 4) % 2,
        slab_index % 4,
    )


def device(xh, core, pz1, pz0, xl, py):
    return (xh * 2 + core, pz1 * 16 + pz0 * 8 + xl * 4 + py)


def block_device(zb, yb):
    return device(zb // 4, yb % 2, yb // 8, (zb // 2) % 2, zb % 2, (yb // 2) % 4)


def scalars(att, penalty, tv_weight, xh):
    rho = penalty[0]
    threshold = tv_weight[0] / rho
    gram = [[None] * 3 for _ in range(3)]
    for i in range(3):
        for j in range(i, 3):
            total = att[0, i] * att[0, j]
            for k in range(1, 8):
                total = total + att[k, i] * att[k, j]
            gram[i][j] = gram[j][i] = total + 12.0 * rho if i == j else total
    cofactor = [
        [
            gram[(r + 1) % 3][(c + 1) % 3] * gram[(r + 2) % 3][(c + 2) % 3]
            - gram[(r + 1) % 3][(c + 2) % 3] * gram[(r + 2) % 3][(c + 1) % 3]
            for c in range(3)
        ]
        for r in range(3)
    ]
    determinant = sum(gram[0][c] * cofactor[0][c] for c in range(3))
    inverse = [[cofactor[c][r] / determinant for c in range(3)] for r in range(3)]
    weight = [
        [sum(inverse[m][n] * att[4 * xh + k, n] for n in range(3)) for k in range(4)]
        for m in range(3)
    ]
    scaled = [[rho * inverse[m][n] for n in range(3)] for m in range(3)]
    return threshold, weight, scaled


def kernel(
    vol, att, penalty, tv_weight, out,
    raw, part, passed, landed, base, field, dual, carry,
    pack_lo, pack_hi, got_lo, got_hi, result,
    load_sem, core_send, core_recv, one_send, one_recv, two_send, two_recv,
    hz_send, hz_recv, hy_send, hy_recv, out_send, out_recv,
):
    xh, core, pz1, pz0, xl, py = position()
    zb = xh * 4 + pz0 * 2 + xl
    yb = pz1 * 8 + py * 2 + core
    partner = device(xh, 1 - core, pz1, pz0, xl, py)
    across = device(xh, core, 1 - pz1, pz0, xl, py)

    def load(q):
        return pltpu.make_async_copy(
            vol.at[:, :, q, core], raw.at[pl.ds(core * 2, 2), :, q], load_sem.at[q]
        )

    def load_body(q, _):
        load(q).start()
        return 0

    lax.fori_loop(0, 8, load_body, 0)

    barrier = pltpu.get_barrier_semaphore()

    def greet(target):
        pl.semaphore_signal(barrier, inc=1, device_id=target, device_id_type=MESH)

    greet(partner)
    greet(across)
    for side in range(2):
        for row in range(4):
            target = device(side, core, pz1, pz0, xl, row)

            @pl.when(jnp.logical_or(side != xh, row != py))
            def _():
                greet(target)

    for dz in (1, 7):
        greet(block_device((zb + dz) % 8, yb))
    for dy in (1, 15):
        greet(block_device(zb, (yb + dy) % 16))

    home = jnp.logical_and(pz0 == core, pz1 == xl)

    def greet_body(y, _):
        source = device(xh, y % 2, y // 8, core, pz1, (y // 2) % 4)

        @pl.when(jnp.logical_not(jnp.logical_and(home, y == yb)))
        def _():
            greet(source)

        return 0

    lax.fori_loop(0, 16, greet_body, 0)

    threshold, weight, scaled = scalars(att, penalty, tv_weight, xh)

    @pl.when(zb == 0)
    def _():
        base[pl.ds(0, HALO)] = jnp.zeros((HALO, 3, 24, NX), F32)

    @pl.when(zb == 7)
    def _():
        base[pl.ds(16 + HALO, HALO)] = jnp.zeros((HALO, 3, 24, NX), F32)

    @pl.when(yb == 0)
    def _():
        got_lo[...] = jnp.zeros_like(got_lo)

    @pl.when(yb == 15)
    def _():
        got_hi[...] = jnp.zeros_like(got_hi)

    pl.semaphore_wait(barrier, 2 + 7 + 4 + 16 - jnp.where(home, 1, 0))

    def swap(q):
        return pltpu.make_async_remote_copy(
            src_ref=vol.at[:, :, q, 1 - core],
            dst_ref=raw.at[pl.ds(core * 2, 2), :, q],
            send_sem=core_send.at[q],
            recv_sem=core_recv.at[q],
            device_id=partner,
            device_id_type=MESH,
        )

    def order(i):
        far = i // 4
        return (far ^ (1 - pz1)) * 4 + (py + i) % 4

    def swap_body(i, _):
        swap(order(i)).start()
        return 0

    lax.fori_loop(0, 8, swap_body, 0)

    def project(q):
        load(q).wait()
        swap(q).wait_recv()

        def body(j, _):
            for r in range(2):
                rows = pl.ds(8 * r, 8)
                bins = [raw[k, j, q, rows, :] for k in range(4)]
                for m in range(3):
                    part[q, j // 2, m, j % 2, rows, :] = (
                        weight[m][0] * bins[0]
                        + weight[m][1] * bins[1]
                        + weight[m][2] * bins[2]
                        + weight[m][3] * bins[3]
                    )
            return 0

        lax.fori_loop(0, 4, body, 0)

    def one(row, h):
        return pltpu.make_async_remote_copy(
            src_ref=part.at[(1 - pz1) * 4 + row, h],
            dst_ref=passed.at[row, h],
            send_sem=one_send.at[row * 2 + h],
            recv_sem=one_recv.at[row * 2 + h],
            device_id=across,
            device_id_type=MESH,
        )

    def one_body(i, _):
        row = (py + i) % 4
        project((1 - pz1) * 4 + row)
        for h in range(2):
            one(row, h).start()
        return 0

    lax.fori_loop(0, 4, one_body, 0)

    def two(source, side, row, h, at):
        return pltpu.make_async_remote_copy(
            src_ref=source,
            dst_ref=landed.at[xh, py, h],
            send_sem=two_send.at[at],
            recv_sem=two_recv.at[xh * 8 + py * 2 + h],
            device_id=device(side, core, pz1, pz0, xl, row),
            device_id_type=MESH,
        )

    def two_local(source, h):
        return pltpu.make_async_copy(
            source, landed.at[xh, py, h], two_recv.at[xh * 8 + py * 2 + h]
        )

    def two_start(source, side, row, h, at):
        mine = jnp.logical_and(side == xh, row == py)

        @pl.when(mine)
        def _():
            two_local(source, h).start()

        @pl.when(jnp.logical_not(mine))
        def _():
            two(source, side, row, h, at).start()

    def own_body(i, _):
        row = (py + i) % 4
        project(pz1 * 4 + row)
        for h in range(2):
            two_start(part.at[pz1 * 4 + row, h], pz1, row, h, row * 2 + h)
        return 0

    lax.fori_loop(0, 4, own_body, 0)

    def pass_body(i, _):
        row = (py + i // 2) % 4
        h = i % 2
        one(row, h).wait_recv()
        two_start(passed.at[row, h], 1 - pz1, row, h, 8 + row * 2 + h)
        return 0

    lax.fori_loop(0, 8, pass_body, 0)

    def reduce_body(i, _):
        row = (py + 4 - i // 2) % 4
        h = i % 2
        for side in range(2):
            pltpu.make_async_remote_copy(
                src_ref=landed.at[side, row, h],
                dst_ref=landed.at[side, row, h],
                send_sem=two_send.at[0],
                recv_sem=two_recv.at[side * 8 + row * 2 + h],
                device_id=partner,
                device_id_type=MESH,
            ).wait_recv()
        for jj in range(2):
            layer = HALO + row * 4 + h * 2 + jj
            for m in range(3):
                base[layer, m, pl.ds(0, 16), :] = (
                    landed[0, row, h, m, jj] + landed[1, row, h, m, jj]
                )
        return 0

    lax.fori_loop(0, 8, reduce_body, 0)

    below = block_device((zb + 7) % 8, yb)
    above = block_device((zb + 1) % 8, yb)
    before = block_device(zb, (yb + 15) % 16)
    after = block_device(zb, (yb + 1) % 16)

    def halo_z(which):
        first, target, place = ((HALO, below, 16 + HALO), (16, above, 0))[which]
        return pltpu.make_async_remote_copy(
            src_ref=base.at[pl.ds(first, HALO), :, pl.ds(0, 16)],
            dst_ref=base.at[pl.ds(place, HALO), :, pl.ds(0, 16)],
            send_sem=hz_send.at[which],
            recv_sem=hz_recv.at[which],
            device_id=target,
            device_id_type=MESH,
        )

    def halo_y(which, late):
        pack, got, target = ((pack_lo, got_hi, before), (pack_hi, got_lo, after))[which]
        rows = pl.ds(8, 3) if late else pl.ds(0, 8)
        return pltpu.make_async_remote_copy(
            src_ref=pack.at[rows],
            dst_ref=got.at[rows],
            send_sem=hy_send.at[which + 2 * late],
            recv_sem=hy_recv.at[which + 2 * late],
            device_id=target,
            device_id_type=MESH,
        )

    has_below, has_above = zb > 0, zb < 7
    has_before, has_after = yb > 0, yb < 15

    @pl.when(has_below)
    def _():
        halo_z(0).start()

    @pl.when(has_above)
    def _():
        halo_z(1).start()

    sub = lax.broadcasted_iota(jnp.int32, (8, NX), 0)

    def pair(i, late):
        return (i, i + 19) if late else (i + HALO, i + HALO + 8)

    def pack_pair(i, late):
        first, second = pair(i, late)
        at = i + 8 if late else i
        for m in range(3):
            lo_first = base[first, m, pl.ds(0, 8), :]
            lo_second = pltpu.roll(base[second, m, pl.ds(0, 8), :], 4, 0)
            pack_lo[at, m] = jnp.where(sub < 4, lo_first, lo_second)
            hi_first = base[first, m, pl.ds(8, 8), :]
            hi_second = pltpu.roll(base[second, m, pl.ds(8, 8), :], 4, 0)
            pack_hi[at, m] = jnp.where(sub < 4, hi_second, hi_first)

    def unpack_pair(i, late):
        first, second = pair(i, late)
        at = i + 8 if late else i
        for m in range(3):
            lo = got_lo[at, m]
            hi = got_hi[at, m]
            base[first, m, pl.ds(16, 8), :] = jnp.where(sub < 4, hi, lo)
            base[second, m, pl.ds(16, 8), :] = pltpu.roll(jnp.where(sub < 4, lo, hi), 4, 0)

    def each_pair(work, late):
        def body(i, _):
            work(i, late)
            return 0

        lax.fori_loop(0, 3 if late else 8, body, 0)

    each_pair(pack_pair, False)

    @pl.when(has_before)
    def _():
        halo_y(0, 0).start()

    @pl.when(has_after)
    def _():
        halo_y(1, 0).start()

    @pl.when(has_above)
    def _():
        halo_z(0).wait_recv()

    @pl.when(has_below)
    def _():
        halo_z(1).wait_recv()

    each_pair(pack_pair, True)

    @pl.when(has_before)
    def _():
        halo_y(0, 1).start()

    @pl.when(has_after)
    def _():
        halo_y(1, 1).start()

    for late in range(2):
        @pl.when(has_after)
        def _():
            halo_y(0, late).wait_recv()

        @pl.when(has_before)
        def _():
            halo_y(1, late).wait_recv()

        each_pair(unpack_pair, late == 1)

    lane = lax.broadcasted_iota(jnp.int32, (8, NX), 1)
    x_mask = jnp.where(lane == NX - 1, 0.0, 1.0).astype(F32)
    y_mask = {
        1: jnp.where(jnp.logical_and(sub == 7, yb == 15), 0.0, 1.0).astype(F32),
        2: jnp.where(jnp.logical_and(sub == 7, yb == 0), 0.0, 1.0).astype(F32),
    }
    limit = threshold * threshold

    def sweep(turn):
        src = base if turn == 0 else field

        def body(z, _):
            z_global = zb * 16 + z - HALO
            z_mask = jnp.where(
                jnp.logical_or(z_global == 127, z_global == -1), 0.0, 1.0
            ).astype(F32)
            here = [[src[z, m, pl.ds(8 * t, 8), :] for m in range(3)] for t in range(3)]
            rolled = [[pltpu.roll(here[t][m], 7, 0) for m in range(3)] for t in range(3)]

            def steps(t):
                rows = pl.ds(8 * t, 8)
                values, old, squares = [], [], None
                for m in range(3):
                    f = here[t][m]
                    along_z = (src[z + 1, m, rows, :] - f) * z_mask
                    along_y = jnp.where(sub == 7, rolled[(t + 1) % 3][m], rolled[t][m]) - f
                    if t:
                        along_y = along_y * y_mask[t]
                    along_x = (pltpu.roll(f, NX - 1, 1) - f) * x_mask
                    triple = [along_z, along_y, along_x]
                    if turn:
                        past = [dual[z, 3 * m + d, rows, :] for d in range(3)]
                        triple = [a + b for a, b in zip(triple, past)]
                        old.append(past)
                    values.append(triple)
                    for v in triple:
                        squares = v * v if squares is None else squares + v * v
                scale = threshold * lax.rsqrt(jnp.maximum(squares, limit))
                twice = scale + scale
                moved = []
                for m in range(3):
                    if turn < 2:
                        for d in range(3):
                            dual[z, 3 * m + d, rows, :] = values[m][d] * scale
                    triple = [v * twice for v in values[m]]
                    if turn:
                        triple = [a - b for a, b in zip(triple, old[m])]
                    moved.append(triple)
                return moved

            def inner(t, moved):
                rows = pl.ds(8 * t, 8)
                partial, turned = [], []
                for m in range(3):
                    step_z, step_y, step_x = moved[m]
                    total = step_z - carry[m, rows, :]
                    carry[m, rows, :] = step_z
                    total = total + (step_x - pltpu.roll(step_x, 1, 1)) + step_y
                    partial.append(total + 12.0 * here[t][m])
                    turned.append(pltpu.roll(step_y, 1, 0))
                return partial, turned

            def finish(t, partial, own, earlier):
                rows = pl.ds(8 * t, 8)
                total = [
                    partial[m] - jnp.where(sub == 0, earlier[m], own[m]) for m in range(3)
                ]
                for m in range(3):
                    value = (
                        base[z, m, rows, :]
                        + scaled[m][0] * total[0]
                        + scaled[m][1] * total[1]
                        + scaled[m][2] * total[2]
                    )
                    if turn < 2:
                        field[z, m, rows, :] = value
                    else:
                        result[z - 2, m, rows, :] = value

            moved = steps(2)
            if turn < 2:
                partial_two, turned_two = inner(2, moved)
            else:
                turned_two = [pltpu.roll(moved[m][1], 1, 0) for m in range(3)]
            partial, turned_zero = inner(0, steps(0))
            finish(0, partial, turned_zero, turned_two)
            partial, turned_one = inner(1, steps(1))
            finish(1, partial, turned_one, turned_zero)
            if turn < 2:
                finish(2, partial_two, turned_two, turned_one)
            return 0

        lax.fori_loop(turn, LAYERS - 1 - turn, body, 0)

    for turn in range(3):
        sweep(turn)

    def send(layer):
        return pltpu.make_async_remote_copy(
            src_ref=result.at[1 + layer],
            dst_ref=out.at[:, pl.ds(pl.multiple_of(yb * 16, 16), 16)],
            send_sem=out_send.at[layer],
            recv_sem=out_recv.at[yb],
            device_id=(xh * 2 + pz0, xl * 16 + layer),
            device_id_type=MESH,
        )

    own_layer = pz0 * 8 + xl * 4 + py

    def send_body(i, _):
        layer = (i + py) % 4 + 4 * ((i // 4) ^ (xl + 2 * pz0))
        mine = jnp.logical_and(home, layer == own_layer)

        @pl.when(mine)
        def _():
            pltpu.make_async_copy(
                result.at[1 + layer],
                out.at[:, pl.ds(pl.multiple_of(yb * 16, 16), 16)],
                out_recv.at[yb],
            ).start()

        @pl.when(jnp.logical_not(mine))
        def _():
            send(layer).start()

        return 0

    lax.fori_loop(0, 16, send_body, 0)

    def drain_swap(q, _):
        swap(q).wait_send()
        one(q // 2, q % 2).wait_send()
        return 0

    lax.fori_loop(0, 8, drain_swap, 0)

    def drain_two(i, _):
        far = i // 8
        row, h = (i // 2) % 4, i % 2
        side = far ^ pz1

        @pl.when(jnp.logical_not(jnp.logical_and(side == xh, row == py)))
        def _():
            two(passed.at[row, h], side, row, h, i).wait_send()

        return 0

    lax.fori_loop(0, 16, drain_two, 0)

    for which in range(2):
        @pl.when((has_below, has_above)[which])
        def _():
            halo_z(which).wait_send()

        @pl.when((has_before, has_after)[which])
        def _():
            halo_y(which, 0).wait_send()
            halo_y(which, 1).wait_send()

    def drain_out(i, _):
        @pl.when(jnp.logical_not(jnp.logical_and(home, i == own_layer)))
        def _():
            send(i).wait_send()

        pltpu.make_async_remote_copy(
            src_ref=result.at[0],
            dst_ref=out.at[:, pl.ds(pl.multiple_of(i * 16, 16), 16)],
            send_sem=out_send.at[0],
            recv_sem=out_recv.at[i],
            device_id=partner,
            device_id_type=MESH,
        ).wait_recv()
        return 0

    lax.fori_loop(0, 16, drain_out, 0)


def on_device(volumes, attenuation, penalty, tv_weight):
    vol = volumes.reshape(2, 4, 8, 2, 16, NX)
    dma = pltpu.SemaphoreType.DMA
    out = pl.pallas_call(
        kernel,
        out_shape=jax.ShapeDtypeStruct((3, 256, NX), F32),
        in_specs=[pl.BlockSpec(memory_space=pl.ANY)]
        + [pl.BlockSpec(memory_space=pltpu.SMEM)] * 3,
        out_specs=pl.BlockSpec(memory_space=pl.ANY),
        scratch_shapes=[
            pltpu.VMEM((4, 4, 8, 16, NX), F32),
            pltpu.VMEM((8, 2, 3, 2, 16, NX), F32),
            pltpu.VMEM((4, 2, 3, 2, 16, NX), F32),
            pltpu.VMEM((2, 4, 2, 3, 2, 16, NX), F32),
            pltpu.VMEM((LAYERS, 3, 24, NX), F32),
            pltpu.VMEM((LAYERS, 3, 24, NX), F32),
            pltpu.VMEM((LAYERS, 9, 24, NX), F32),
            pltpu.VMEM((3, 24, NX), F32),
            pltpu.VMEM((11, 3, 8, NX), F32),
            pltpu.VMEM((11, 3, 8, NX), F32),
            pltpu.VMEM((11, 3, 8, NX), F32),
            pltpu.VMEM((11, 3, 8, NX), F32),
            pltpu.VMEM((17, 3, 16, NX), F32),
            dma((8,)), dma((8,)), dma((8,)),
            dma((8,)), dma((8,)),
            dma((16,)), dma((16,)),
            dma((2,)), dma((2,)), dma((4,)), dma((4,)),
            dma((16,)), dma((16,)),
        ],
        compiler_params=pltpu.CompilerParams(
            collective_id=0, has_side_effects=True, vmem_limit_bytes=56 * 1024 * 1024
        ),
        cost_estimate=pl.CostEstimate(
            flops=60_000_000, bytes_accessed=8_000_000, transcendentals=400_000
        ),
    )(vol, attenuation, penalty, tv_weight)
    return out.reshape(3, 1, 256, NX)


def solution(mesh):
    placed = (P("bin", "slab", None, None), P(), P(), P())
    return jax.shard_map(
        on_device,
        mesh=mesh,
        in_specs=placed,
        out_specs=P(None, ("bin", "slab"), None, None),
        check_vma=False,
    )
```

profile of v0, /device:TPU:67, one launch (start us, length us, event | category | flops | bytes accessed | tf_op | source)
XLA Modules:
  0.0 134.9 jit_solution(14596110867275878960)
XLA Ops:
  1.3 1.3 copy.5.att
  2.6 129.6 %shard_map.46 = f32[3,256,512]{2,1,0:T(8,128)} custom-call(f32[2,4,8,2,16,512]{5,4,3,2,1,0:T(8,128)} %bitcast.5, f32[8,3]{1,0:T(8,128)} %copy.5.att, f32[1]{0:T(128)S(6)} %copy.8.penalty, f32[1]{0:T(128)S(6)} %copy.9.tv_weight), custom_call_target="tpu_custom_call" | custom-call | flops 60000000 | bytes 8000000 | tf_op jit(solution)/shard_map/pallas_call | solution.py:555
  132.2 2.7 %copy.10 = f32[3,1,256,512]{3,2,1,0:T(8,128)} copy(f32[3,1,256,512]{3,2,1,0:T(8,128)} %bitcast.4) | data formatting | bytes 3145728
where the time goes:
time: 135 us
  Pallas kernels  130 us (96%)
  local copies, waits for them, and re-layouts  4.02 us (3%)
    pallas_call x1, Pallas kernels, on_device(): pl.pallas_call(kernel, out_shape=jax.ShapeDtypeStruct((3, 256, NX), F32),...  130 us
    unnamed x2, local copies, waits for them, and re-layouts  4.02 us

commit v1 on v0

--- a/solution.py
+++ b/solution.py
@@ -10,6 +10,8 @@
 HALO = 3
 LAYERS = 16 + 2 * HALO
 NX = 512
+LAG = 4
+PIECES = 16
 
 
 def position():
@@ -74,13 +76,17 @@
     partner = device(xh, 1 - core, pz1, pz0, xl, py)
     across = device(xh, core, 1 - pz1, pz0, xl, py)
 
-    def load(q):
+    def bins_at(n):
+        return n // 2, pl.ds(((1 - n % 2) ^ pz1) * 4, 4)
+
+    def load(n):
+        layer, rows = bins_at(n)
         return pltpu.make_async_copy(
-            vol.at[:, :, q, core], raw.at[pl.ds(core * 2, 2), :, q], load_sem.at[q]
+            vol.at[:, layer, rows, core], raw.at[pl.ds(core * 2, 2), layer, rows], load_sem.at[n]
         )
 
-    def load_body(q, _):
-        load(q).start()
+    def load_body(n, _):
+        load(n).start()
         return 0
 
     lax.fori_loop(0, 8, load_body, 0)
@@ -138,36 +144,41 @@
 
     pl.semaphore_wait(barrier, 2 + 7 + 4 + 16 - jnp.where(home, 1, 0))
 
-    def swap(q):
+    def swap(n):
+        layer, rows = bins_at(n)
         return pltpu.make_async_remote_copy(
-            src_ref=vol.at[:, :, q, 1 - core],
-            dst_ref=raw.at[pl.ds(core * 2, 2), :, q],
-            send_sem=core_send.at[q],
-            recv_sem=core_recv.at[q],
+            src_ref=vol.at[:, layer, rows, 1 - core],
+            dst_ref=raw.at[pl.ds(core * 2, 2), layer, rows],
+            send_sem=core_send.at[n],
+            recv_sem=core_recv.at[n],
             device_id=partner,
             device_id_type=MESH,
         )
 
-    def order(i):
-        far = i // 4
-        return (far ^ (1 - pz1)) * 4 + (py + i) % 4
-
-    def swap_body(i, _):
-        swap(order(i)).start()
-        return 0
-
-    lax.fori_loop(0, 8, swap_body, 0)
-
-    def project(q):
-        load(q).wait()
-        swap(q).wait_recv()
-
-        def body(j, _):
+    def swap_body(n, _):
+        swap(n).start()
+        return 0
+
+    lax.fori_loop(0, 4, swap_body, 0)
+
+    def project(n):
+        load(n).wait()
+        swap(n).wait_recv()
+
+        @pl.when(n < 4)
+        def _():
+            swap(n + 4).start()
+
+        layer = n // 2
+        first = ((1 - n % 2) ^ pz1) * 4
+
+        def body(k, _):
+            q = first + k
             for r in range(2):
                 rows = pl.ds(8 * r, 8)
-                bins = [raw[k, j, q, rows, :] for k in range(4)]
+                bins = [raw[b, layer, q, rows, :] for b in range(4)]
                 for m in range(3):
-                    part[q, j // 2, m, j % 2, rows, :] = (
+                    part[q, layer, m, rows, :] = (
                         weight[m][0] * bins[0]
                         + weight[m][1] * bins[1]
                         + weight[m][2] * bins[2]
@@ -177,90 +188,104 @@
 
         lax.fori_loop(0, 4, body, 0)
 
-    def one(row, h):
+    def ahead(i):
+        k = i % 4
+        return jnp.where(k < 2, 2 * k + 1, 6 - 2 * k)
+
+    def piece(i):
+        return (py + ahead(i)) % 4, i // 4
+
+    def one(i):
+        row, h = piece(i)
         return pltpu.make_async_remote_copy(
             src_ref=part.at[(1 - pz1) * 4 + row, h],
             dst_ref=passed.at[row, h],
-            send_sem=one_send.at[row * 2 + h],
-            recv_sem=one_recv.at[row * 2 + h],
+            send_sem=one_send.at[i],
+            recv_sem=one_recv.at[i],
             device_id=across,
             device_id_type=MESH,
         )
 
-    def one_body(i, _):
-        row = (py + i) % 4
-        project((1 - pz1) * 4 + row)
-        for h in range(2):
-            one(row, h).start()
-        return 0
-
-    lax.fori_loop(0, 4, one_body, 0)
-
-    def two(source, side, row, h, at):
+    def two(i, passing):
+        row, h = piece(i)
+        source = passed.at[row, h] if passing else part.at[pz1 * 4 + row, h]
         return pltpu.make_async_remote_copy(
             src_ref=source,
             dst_ref=landed.at[xh, py, h],
-            send_sem=two_send.at[at],
-            recv_sem=two_recv.at[xh * 8 + py * 2 + h],
-            device_id=device(side, core, pz1, pz0, xl, row),
+            send_sem=two_send.at[i + PIECES * passing],
+            recv_sem=two_recv.at[(xh * 4 + py) * 4 + h],
+            device_id=device(1 - pz1 if passing else pz1, core, pz1, pz0, xl, row),
             device_id_type=MESH,
         )
 
-    def two_local(source, h):
-        return pltpu.make_async_copy(
-            source, landed.at[xh, py, h], two_recv.at[xh * 8 + py * 2 + h]
-        )
-
-    def two_start(source, side, row, h, at):
-        mine = jnp.logical_and(side == xh, row == py)
-
-        @pl.when(mine)
-        def _():
-            two_local(source, h).start()
-
-        @pl.when(jnp.logical_not(mine))
-        def _():
-            two(source, side, row, h, at).start()
-
-    def own_body(i, _):
-        row = (py + i) % 4
-        project(pz1 * 4 + row)
-        for h in range(2):
-            two_start(part.at[pz1 * 4 + row, h], pz1, row, h, row * 2 + h)
-        return 0
-
-    lax.fori_loop(0, 4, own_body, 0)
-
-    def pass_body(i, _):
-        row = (py + i // 2) % 4
-        h = i % 2
-        one(row, h).wait_recv()
-        two_start(passed.at[row, h], 1 - pz1, row, h, 8 + row * 2 + h)
-        return 0
-
-    lax.fori_loop(0, 8, pass_body, 0)
+    def two_stays(i, passing):
+        return jnp.logical_and(xh == (1 - pz1 if passing else pz1), ahead(i) == 0)
+
+    def two_start(i, passing):
+        row, h = piece(i)
+        stays = two_stays(i, passing)
+        source = passed.at[row, h] if passing else part.at[pz1 * 4 + row, h]
+
+        @pl.when(stays)
+        def _():
+            pltpu.make_async_copy(
+                source, landed.at[xh, py, h], two_recv.at[(xh * 4 + py) * 4 + h]
+            ).start()
+
+        @pl.when(jnp.logical_not(stays))
+        def _():
+            two(i, passing).start()
+
+    def two_sent(i, passing):
+        @pl.when(jnp.logical_not(two_stays(i, passing)))
+        def _():
+            two(i, passing).wait_send()
+
+    def pass_on(i):
+        one(i).wait_recv()
+        two_start(i, 1)
+
+    def input_body(i, _):
+        @pl.when(i % 4 == 0)
+        def _():
+            project(i // 2)
+            project(i // 2 + 1)
+
+        one(i).start()
+        two_start(i, 0)
+
+        @pl.when(i >= LAG)
+        def _():
+            pass_on(i - LAG)
+
+        return 0
+
+    lax.fori_loop(0, PIECES, input_body, 0)
+
+    def tail_body(i, _):
+        pass_on(i)
+        return 0
+
+    lax.fori_loop(PIECES - LAG, PIECES, tail_body, 0)
 
     def reduce_body(i, _):
-        row = (py + 4 - i // 2) % 4
-        h = i % 2
+        row = (py + 4 - ahead(i)) % 4
+        h = i // 4
         for side in range(2):
             pltpu.make_async_remote_copy(
                 src_ref=landed.at[side, row, h],
                 dst_ref=landed.at[side, row, h],
                 send_sem=two_send.at[0],
-                recv_sem=two_recv.at[side * 8 + row * 2 + h],
+                recv_sem=two_recv.at[(side * 4 + row) * 4 + h],
                 device_id=partner,
                 device_id_type=MESH,
             ).wait_recv()
-        for jj in range(2):
-            layer = HALO + row * 4 + h * 2 + jj
-            for m in range(3):
-                base[layer, m, pl.ds(0, 16), :] = (
-                    landed[0, row, h, m, jj] + landed[1, row, h, m, jj]
-                )
-        return 0
-
-    lax.fori_loop(0, 8, reduce_body, 0)
+        layer = HALO + row * 4 + h
+        for m in range(3):
+            base[layer, m, pl.ds(0, 16), :] = landed[0, row, h, m] + landed[1, row, h, m]
+        return 0
+
+    lax.fori_loop(0, PIECES, reduce_body, 0)
 
     below = block_device((zb + 7) % 8, yb)
     above = block_device((zb + 1) % 8, yb)
@@ -503,23 +528,17 @@
 
     def drain_swap(q, _):
         swap(q).wait_send()
-        one(q // 2, q % 2).wait_send()
         return 0
 
     lax.fori_loop(0, 8, drain_swap, 0)
 
     def drain_two(i, _):
-        far = i // 8
-        row, h = (i // 2) % 4, i % 2
-        side = far ^ pz1
-
-        @pl.when(jnp.logical_not(jnp.logical_and(side == xh, row == py)))
-        def _():
-            two(passed.at[row, h], side, row, h, i).wait_send()
-
-        return 0
-
-    lax.fori_loop(0, 16, drain_two, 0)
+        one(i).wait_send()
+        two_sent(i, 0)
+        two_sent(i, 1)
+        return 0
+
+    lax.fori_loop(0, PIECES, drain_two, 0)
 
     for which in range(2):
         @pl.when((has_below, has_above)[which])
@@ -560,9 +579,9 @@
         out_specs=pl.BlockSpec(memory_space=pl.ANY),
         scratch_shapes=[
             pltpu.VMEM((4, 4, 8, 16, NX), F32),
-            pltpu.VMEM((8, 2, 3, 2, 16, NX), F32),
-            pltpu.VMEM((4, 2, 3, 2, 16, NX), F32),
-            pltpu.VMEM((2, 4, 2, 3, 2, 16, NX), F32),
+            pltpu.VMEM((8, 4, 3, 16, NX), F32),
+            pltpu.VMEM((4, 4, 3, 16, NX), F32),
+            pltpu.VMEM((2, 4, 4, 3, 16, NX), F32),
             pltpu.VMEM((LAYERS, 3, 24, NX), F32),
             pltpu.VMEM((LAYERS, 3, 24, NX), F32),
             pltpu.VMEM((LAYERS, 9, 24, NX), F32),
@@ -573,8 +592,8 @@
             pltpu.VMEM((11, 3, 8, NX), F32),
             pltpu.VMEM((17, 3, 16, NX), F32),
             dma((8,)), dma((8,)), dma((8,)),
-            dma((8,)), dma((8,)),
-            dma((16,)), dma((16,)),
+            dma((PIECES,)), dma((PIECES,)),
+            dma((2 * PIECES,)), dma((2 * PIECES,)),
             dma((2,)), dma((2,)), dma((4,)), dma((4,)),
             dma((16,)), dma((16,)),
         ],

time: 135 us -> 118 us (0.87)
  the two profiles are of different devices: /device:TPU:67 before, /device:TPU:3 now
where the time goes in v1:
time: 118 us
  Pallas kernels  112 us (95%)
  local copies, waits for them, and re-layouts  4.02 us (3%)
  between operations  1.31 us (1%)
    pallas_call x1, Pallas kernels, on_device(): pl.pallas_call(kernel, out_shape=jax.ShapeDtypeStruct((3, 256, NX), F32),...  112 us
    unnamed x2, local copies, waits for them, and re-layouts  4.02 us

profile of v1, /device:TPU:3, one launch (start us, length us, event | category | flops | bytes accessed | tf_op | source)
XLA Modules:
  0.0 117.7 jit_solution(14003882743737325960)
XLA Ops:
  1.3 1.3 %copy.5.att = f32[8,3]{1,0:T(8,128)} copy(f32[8,3]{0,1:T(4,128)} %param.5) | data formatting | bytes 192 | tf_op args[1]
  2.6 112.4 %shard_map.46 = f32[3,256,512]{2,1,0:T(8,128)} custom-call(f32[2,4,8,2,16,512]{5,4,3,2,1,0:T(8,128)} %bitcast.5, f32[8,3]{1,0:T(8,128)} %copy.5.att, f32[1]{0:T(128)S(6)} %copy.8.penalty, f32[1]{0:T(128)S(6)} %copy.9.tv_weight), custom_call_target="tpu_custom_call" | custom-call | flops 60000000 | bytes 8000000 | tf_op jit(solution)/shard_map/pallas_call | solution.py:574
  115.1 2.7 %copy.10 = f32[3,1,256,512]{3,2,1,0:T(8,128)} copy(f32[3,1,256,512]{3,2,1,0:T(8,128)} %bitcast.4) | data formatting | bytes 3145728

commit v2 on v1

--- a/solution.py
+++ b/solution.py
@@ -32,7 +32,8 @@
 
 
 def block_device(zb, yb):
-    return device(zb // 4, yb % 2, yb // 8, (zb // 2) % 2, zb % 2, (yb // 2) % 4)
+    pz0 = (zb // 2) % 2
+    return device(zb // 4, yb % 2, yb // 8, pz0, (zb % 2) ^ pz0, (yb // 2) % 4)
 
 
 def scalars(att, penalty, tv_weight, xh):
@@ -41,9 +42,9 @@
     gram = [[None] * 3 for _ in range(3)]
     for i in range(3):
         for j in range(i, 3):
-            total = att[0, i] * att[0, j]
+            total = att[i, 0] * att[j, 0]
             for k in range(1, 8):
-                total = total + att[k, i] * att[k, j]
+                total = total + att[i, k] * att[j, k]
             gram[i][j] = gram[j][i] = total + 12.0 * rho if i == j else total
     cofactor = [
         [
@@ -56,7 +57,7 @@
     determinant = sum(gram[0][c] * cofactor[0][c] for c in range(3))
     inverse = [[cofactor[c][r] / determinant for c in range(3)] for r in range(3)]
     weight = [
-        [sum(inverse[m][n] * att[4 * xh + k, n] for n in range(3)) for k in range(4)]
+        [sum(inverse[m][n] * att[n, 4 * xh + k] for n in range(3)) for k in range(4)]
         for m in range(3)
     ]
     scaled = [[rho * inverse[m][n] for n in range(3)] for m in range(3)]
@@ -65,13 +66,14 @@
 
 def kernel(
     vol, att, penalty, tv_weight, out,
-    raw, part, passed, landed, base, field, dual, carry,
+    raw, part, passed, landed, base, field_one, field_two, dual_zero, dual_one, carry,
     pack_lo, pack_hi, got_lo, got_hi, result,
     load_sem, core_send, core_recv, one_send, one_recv, two_send, two_recv,
     hz_send, hz_recv, hy_send, hy_recv, out_send, out_recv,
 ):
     xh, core, pz1, pz0, xl, py = position()
-    zb = xh * 4 + pz0 * 2 + xl
+    turned_xl = xl ^ pz0
+    zb = xh * 4 + pz0 * 2 + turned_xl
     yb = pz1 * 8 + py * 2 + core
     partner = device(xh, 1 - core, pz1, pz0, xl, py)
     across = device(xh, core, 1 - pz1, pz0, xl, py)
@@ -100,9 +102,9 @@
     greet(across)
     for side in range(2):
         for row in range(4):
-            target = device(side, core, pz1, pz0, xl, row)
-
-            @pl.when(jnp.logical_or(side != xh, row != py))
+            target = device(side, core, pz1, pz0, turned_xl, row)
+
+            @pl.when(jnp.logical_or(jnp.logical_or(side != xh, row != py), pz0 == 1))
             def _():
                 greet(target)
 
@@ -111,10 +113,10 @@
     for dy in (1, 15):
         greet(block_device(zb, (yb + dy) % 16))
 
-    home = jnp.logical_and(pz0 == core, pz1 == xl)
+    home = jnp.logical_and(pz0 == core, pz1 == turned_xl)
 
     def greet_body(y, _):
-        source = device(xh, y % 2, y // 8, core, pz1, (y // 2) % 4)
+        source = device(xh, y % 2, y // 8, core, pz1 ^ core, (y // 2) % 4)
 
         @pl.when(jnp.logical_not(jnp.logical_and(home, y == yb)))
         def _():
@@ -142,7 +144,7 @@
     def _():
         got_hi[...] = jnp.zeros_like(got_hi)
 
-    pl.semaphore_wait(barrier, 2 + 7 + 4 + 16 - jnp.where(home, 1, 0))
+    pl.semaphore_wait(barrier, 2 + 7 + pz0 + 4 + 16 - jnp.where(home, 1, 0))
 
     def swap(n):
         layer, rows = bins_at(n)
@@ -214,12 +216,13 @@
             dst_ref=landed.at[xh, py, h],
             send_sem=two_send.at[i + PIECES * passing],
             recv_sem=two_recv.at[(xh * 4 + py) * 4 + h],
-            device_id=device(1 - pz1 if passing else pz1, core, pz1, pz0, xl, row),
+            device_id=device(1 - pz1 if passing else pz1, core, pz1, pz0, turned_xl, row),
             device_id_type=MESH,
         )
 
     def two_stays(i, passing):
-        return jnp.logical_and(xh == (1 - pz1 if passing else pz1), ahead(i) == 0)
+        same = jnp.logical_and(xh == (1 - pz1 if passing else pz1), ahead(i) == 0)
+        return jnp.logical_and(same, pz0 == 0)
 
     def two_start(i, passing):
         row, h = piece(i)
@@ -268,72 +271,47 @@
 
     lax.fori_loop(PIECES - LAG, PIECES, tail_body, 0)
 
-    def reduce_body(i, _):
-        row = (py + 4 - ahead(i)) % 4
-        h = i // 4
-        for side in range(2):
-            pltpu.make_async_remote_copy(
-                src_ref=landed.at[side, row, h],
-                dst_ref=landed.at[side, row, h],
-                send_sem=two_send.at[0],
-                recv_sem=two_recv.at[(side * 4 + row) * 4 + h],
-                device_id=partner,
-                device_id_type=MESH,
-            ).wait_recv()
-        layer = HALO + row * 4 + h
-        for m in range(3):
-            base[layer, m, pl.ds(0, 16), :] = landed[0, row, h, m] + landed[1, row, h, m]
-        return 0
-
-    lax.fori_loop(0, PIECES, reduce_body, 0)
-
     below = block_device((zb + 7) % 8, yb)
     above = block_device((zb + 1) % 8, yb)
     before = block_device(zb, (yb + 15) % 16)
     after = block_device(zb, (yb + 1) % 16)
-
-    def halo_z(which):
+    has_below, has_above = zb > 0, zb < 7
+    has_before, has_after = yb > 0, yb < 15
+
+    def halo_z(which, n):
         first, target, place = ((HALO, below, 16 + HALO), (16, above, 0))[which]
         return pltpu.make_async_remote_copy(
-            src_ref=base.at[pl.ds(first, HALO), :, pl.ds(0, 16)],
-            dst_ref=base.at[pl.ds(place, HALO), :, pl.ds(0, 16)],
-            send_sem=hz_send.at[which],
-            recv_sem=hz_recv.at[which],
+            src_ref=base.at[first + n, :, pl.ds(0, 16)],
+            dst_ref=base.at[place + n, :, pl.ds(0, 16)],
+            send_sem=hz_send.at[which * 3 + n],
+            recv_sem=hz_recv.at[which * 3 + n],
             device_id=target,
             device_id_type=MESH,
         )
 
-    def halo_y(which, late):
+    def halo_y(which, n):
         pack, got, target = ((pack_lo, got_hi, before), (pack_hi, got_lo, after))[which]
-        rows = pl.ds(8, 3) if late else pl.ds(0, 8)
+        late = isinstance(n, int) and n == 4
+        rows = pl.ds(8, 3) if late else pl.ds(2 * n, 2)
         return pltpu.make_async_remote_copy(
             src_ref=pack.at[rows],
             dst_ref=got.at[rows],
-            send_sem=hy_send.at[which + 2 * late],
-            recv_sem=hy_recv.at[which + 2 * late],
+            send_sem=hy_send.at[which * 5 + n],
+            recv_sem=hy_recv.at[which * 5 + n],
             device_id=target,
             device_id_type=MESH,
         )
 
-    has_below, has_above = zb > 0, zb < 7
-    has_before, has_after = yb > 0, yb < 15
-
-    @pl.when(has_below)
-    def _():
-        halo_z(0).start()
-
-    @pl.when(has_above)
-    def _():
-        halo_z(1).start()
-
     sub = lax.broadcasted_iota(jnp.int32, (8, NX), 0)
 
-    def pair(i, late):
-        return (i, i + 19) if late else (i + HALO, i + HALO + 8)
-
-    def pack_pair(i, late):
-        first, second = pair(i, late)
-        at = i + 8 if late else i
+    def pair(at, late):
+        if late:
+            return at - 8, at + 11
+        first = HALO + at // 2 + 4 * (at % 2)
+        return first, first + 8
+
+    def pack_pair(at, late):
+        first, second = pair(at, late)
         for m in range(3):
             lo_first = base[first, m, pl.ds(0, 8), :]
             lo_second = pltpu.roll(base[second, m, pl.ds(0, 8), :], 4, 0)
@@ -342,60 +320,72 @@
             hi_second = pltpu.roll(base[second, m, pl.ds(8, 8), :], 4, 0)
             pack_hi[at, m] = jnp.where(sub < 4, hi_second, hi_first)
 
-    def unpack_pair(i, late):
-        first, second = pair(i, late)
-        at = i + 8 if late else i
+    def unpack_pair(at, late):
+        first, second = pair(at, late)
         for m in range(3):
             lo = got_lo[at, m]
             hi = got_hi[at, m]
             base[first, m, pl.ds(16, 8), :] = jnp.where(sub < 4, hi, lo)
             base[second, m, pl.ds(16, 8), :] = pltpu.roll(jnp.where(sub < 4, lo, hi), 4, 0)
 
-    def each_pair(work, late):
-        def body(i, _):
-            work(i, late)
+    def reduce_body(h, _):
+        def piece_body(k, _):
+            row = (py + 4 - ahead(k)) % 4
+            for side in range(2):
+                pltpu.make_async_remote_copy(
+                    src_ref=landed.at[side, row, h],
+                    dst_ref=landed.at[side, row, h],
+                    send_sem=two_send.at[0],
+                    recv_sem=two_recv.at[(side * 4 + row) * 4 + h],
+                    device_id=partner,
+                    device_id_type=MESH,
+                ).wait_recv()
+            layer = HALO + row * 4 + h
+            for m in range(3):
+                base[layer, m, pl.ds(0, 16), :] = landed[0, row, h, m] + landed[1, row, h, m]
             return 0
 
-        lax.fori_loop(0, 3 if late else 8, body, 0)
-
-    each_pair(pack_pair, False)
-
-    @pl.when(has_before)
-    def _():
-        halo_y(0, 0).start()
-
-    @pl.when(has_after)
-    def _():
-        halo_y(1, 0).start()
-
-    @pl.when(has_above)
-    def _():
-        halo_z(0).wait_recv()
-
-    @pl.when(has_below)
-    def _():
-        halo_z(1).wait_recv()
-
-    each_pair(pack_pair, True)
-
-    @pl.when(has_before)
-    def _():
-        halo_y(0, 1).start()
-
-    @pl.when(has_after)
-    def _():
-        halo_y(1, 1).start()
-
-    for late in range(2):
+        lax.fori_loop(0, 4, piece_body, 0)
+
+        @pl.when(jnp.logical_and(has_below, h < 3))
+        def _():
+            halo_z(0, h).start()
+
+        @pl.when(jnp.logical_and(has_above, h > 0))
+        def _():
+            halo_z(1, h - 1).start()
+
+        for half in range(2):
+            pack_pair(2 * h + half, False)
+
+        @pl.when(has_before)
+        def _():
+            halo_y(0, h).start()
+
         @pl.when(has_after)
         def _():
-            halo_y(0, late).wait_recv()
+            halo_y(1, h).start()
+
+        return 0
+
+    lax.fori_loop(0, 4, reduce_body, 0)
+
+    def arrive_y(n):
+        @pl.when(has_after)
+        def _():
+            halo_y(0, n).wait_recv()
 
         @pl.when(has_before)
         def _():
-            halo_y(1, late).wait_recv()
-
-        each_pair(unpack_pair, late == 1)
+            halo_y(1, n).wait_recv()
+
+    def arrive_body(h, _):
+        arrive_y(h)
+        for half in range(2):
+            unpack_pair(2 * h + half, False)
+        return 0
+
+    lax.fori_loop(0, 4, arrive_body, 0)
 
     lane = lax.broadcasted_iota(jnp.int32, (8, NX), 1)
     x_mask = jnp.where(lane == NX - 1, 0.0, 1.0).astype(F32)
@@ -405,8 +395,11 @@
     }
     limit = threshold * threshold
 
-    def sweep(turn):
-        src = base if turn == 0 else field
+    def sweep(turn, first, last):
+        src = (base, field_one, field_two)[turn]
+        target = (field_one, field_two, result)[turn]
+        dual = (dual_zero, dual_one, None)[turn]
+        dual_past = (None, dual_zero, dual_one)[turn]
 
         def body(z, _):
             z_global = zb * 16 + z - HALO
@@ -428,7 +421,7 @@
                     along_x = (pltpu.roll(f, NX - 1, 1) - f) * x_mask
                     triple = [along_z, along_y, along_x]
                     if turn:
-                        past = [dual[z, 3 * m + d, rows, :] for d in range(3)]
+                        past = [dual_past[z, 3 * m + d, rows, :] for d in range(3)]
                         triple = [a + b for a, b in zip(triple, past)]
                         old.append(past)
                     values.append(triple)
@@ -452,8 +445,8 @@
                 partial, turned = [], []
                 for m in range(3):
                     step_z, step_y, step_x = moved[m]
-                    total = step_z - carry[m, rows, :]
-                    carry[m, rows, :] = step_z
+                    total = step_z - carry[turn, m, rows, :]
+                    carry[turn, m, rows, :] = step_z
                     total = total + (step_x - pltpu.roll(step_x, 1, 1)) + step_y
                     partial.append(total + 12.0 * here[t][m])
                     turned.append(pltpu.roll(step_y, 1, 0))
@@ -471,10 +464,7 @@
                         + scaled[m][1] * total[1]
                         + scaled[m][2] * total[2]
                     )
-                    if turn < 2:
-                        field[z, m, rows, :] = value
-                    else:
-                        result[z - 2, m, rows, :] = value
+                    target[z - 2 if turn == 2 else z, m, rows, :] = value
 
             moved = steps(2)
             if turn < 2:
@@ -489,10 +479,7 @@
                 finish(2, partial_two, turned_two, turned_one)
             return 0
 
-        lax.fori_loop(turn, LAYERS - 1 - turn, body, 0)
-
-    for turn in range(3):
-        sweep(turn)
+        lax.fori_loop(first, last + 1, body, 0)
 
     def send(layer):
         return pltpu.make_async_remote_copy(
@@ -500,14 +487,13 @@
             dst_ref=out.at[:, pl.ds(pl.multiple_of(yb * 16, 16), 16)],
             send_sem=out_send.at[layer],
             recv_sem=out_recv.at[yb],
-            device_id=(xh * 2 + pz0, xl * 16 + layer),
+            device_id=(xh * 2 + pz0, turned_xl * 16 + layer),
             device_id_type=MESH,
         )
 
     own_layer = pz0 * 8 + xl * 4 + py
 
-    def send_body(i, _):
-        layer = (i + py) % 4 + 4 * ((i // 4) ^ (xl + 2 * pz0))
+    def send_layer(layer):
         mine = jnp.logical_and(home, layer == own_layer)
 
         @pl.when(mine)
@@ -522,9 +508,51 @@
         def _():
             send(layer).start()
 
-        return 0
-
-    lax.fori_loop(0, 16, send_body, 0)
+    spread = py + 4 * (xl + 2 * pz0)
+
+    def send_inner(i, _):
+        send_layer(3 + (i + spread) % 10)
+        return 0
+
+    def send_outer(i, _):
+        k = (i + spread) % 6
+        send_layer(jnp.where(k < 3, k, k + 10))
+        return 0
+
+    sweep(0, 3, 17)
+    for n in range(3):
+        @pl.when(has_above)
+        def _():
+            halo_z(0, n).wait_recv()
+
+        @pl.when(has_below)
+        def _():
+            halo_z(1, n).wait_recv()
+
+    for at in range(8, 11):
+        pack_pair(at, True)
+
+    @pl.when(has_before)
+    def _():
+        halo_y(0, 4).start()
+
+    @pl.when(has_after)
+    def _():
+        halo_y(1, 4).start()
+
+    sweep(1, 4, 16)
+    sweep(2, 5, 15)
+    lax.fori_loop(0, 10, send_inner, 0)
+    arrive_y(4)
+    for at in range(8, 11):
+        unpack_pair(at, True)
+    sweep(0, 18, 20)
+    sweep(0, 0, 3)
+    sweep(1, 17, 19)
+    sweep(1, 1, 4)
+    sweep(2, 16, 18)
+    sweep(2, 2, 5)
+    lax.fori_loop(0, 6, send_outer, 0)
 
     def drain_swap(q, _):
         swap(q).wait_send()
@@ -543,12 +571,13 @@
     for which in range(2):
         @pl.when((has_below, has_above)[which])
         def _():
-            halo_z(which).wait_send()
+            for n in range(3):
+                halo_z(which, n).wait_send()
 
         @pl.when((has_before, has_after)[which])
         def _():
-            halo_y(which, 0).wait_send()
-            halo_y(which, 1).wait_send()
+            for n in range(5):
+                halo_y(which, n).wait_send()
 
     def drain_out(i, _):
         @pl.when(jnp.logical_not(jnp.logical_and(home, i == own_layer)))
@@ -584,8 +613,10 @@
             pltpu.VMEM((2, 4, 4, 3, 16, NX), F32),
             pltpu.VMEM((LAYERS, 3, 24, NX), F32),
             pltpu.VMEM((LAYERS, 3, 24, NX), F32),
+            pltpu.VMEM((LAYERS, 3, 24, NX), F32),
             pltpu.VMEM((LAYERS, 9, 24, NX), F32),
-            pltpu.VMEM((3, 24, NX), F32),
+            pltpu.VMEM((LAYERS, 9, 24, NX), F32),
+            pltpu.VMEM((3, 3, 24, NX), F32),
             pltpu.VMEM((11, 3, 8, NX), F32),
             pltpu.VMEM((11, 3, 8, NX), F32),
             pltpu.VMEM((11, 3, 8, NX), F32),
@@ -594,16 +625,16 @@
             dma((8,)), dma((8,)), dma((8,)),
             dma((PIECES,)), dma((PIECES,)),
             dma((2 * PIECES,)), dma((2 * PIECES,)),
-            dma((2,)), dma((2,)), dma((4,)), dma((4,)),
+            dma((6,)), dma((6,)), dma((10,)), dma((10,)),
             dma((16,)), dma((16,)),
         ],
         compiler_params=pltpu.CompilerParams(
-            collective_id=0, has_side_effects=True, vmem_limit_bytes=56 * 1024 * 1024
+            collective_id=0, has_side_effects=True, vmem_limit_bytes=51 * 1024 * 1024
         ),
         cost_estimate=pl.CostEstimate(
             flops=60_000_000, bytes_accessed=8_000_000, transcendentals=400_000
         ),
-    )(vol, attenuation, penalty, tv_weight)
+    )(vol, attenuation.T, penalty, tv_weight)
     return out.reshape(3, 1, 256, NX)
 
 

time: 118 us -> 106 us (0.90)
  the two profiles are of different devices: /device:TPU:3 before, /device:TPU:9 now
where the time goes in v2:
time: 106 us; the launch traced here: 105 us
  Pallas kernels  102 us (96%)
  local copies, waits for them, and re-layouts  1.82 us (2%)
  between operations  1.31 us (1%)
    pallas_call x1, Pallas kernels, on_device(): pl.pallas_call(kernel, out_shape=jax.ShapeDtypeStruct((3, 256, NX), F32),...  102 us

profile of v2, /device:TPU:9, one launch (start us, length us, event | category | flops | bytes accessed | tf_op | source)
XLA Modules:
  0.0 105.4 jit_solution(2460590735555631140)
XLA Ops:
  1.3 0.0 copy-start
  1.3 0.7 copy-done
  2.0 102.3 %shard_map.46 = f32[3,256,512]{2,1,0:T(8,128)S(1)} custom-call(f32[2,4,8,2,16,512]{5,4,3,2,1,0:T(8,128)} %bitcast.7, f32[3,8]{1,0:T(4,128)S(1)} %bitcast.6, f32[1]{0:T(128)S(6)} %copy.7.penalty, f32[1]{0:T(128)S(6)} %copy.8.tv_weight), custom_call_target="tpu_custom_call" | custom-call | flops 60000000 | bytes 8000000 | tf_op jit(solution)/shard_map/pallas_call | solution.py:603
  104.3 1.1 %copy.9 = f32[3,1,256,512]{3,2,1,0:T(8,128)} copy(f32[3,1,256,512]{3,2,1,0:T(8,128)S(1)} %bitcast.5) | data formatting | bytes 3145728
Async XLA Ops:
  1.3 0.7 copy-start

commit v3 on v2

--- a/solution.py
+++ b/solution.py
@@ -66,7 +66,7 @@
 
 def kernel(
     vol, att, penalty, tv_weight, out,
-    raw, part, passed, landed, base, field_one, field_two, dual_zero, dual_one, carry,
+    raw, part, passed, landed, base, field_one, field_two, dual_zero, dual_one, div_zero, div_one, carry,
     pack_lo, pack_hi, got_lo, got_hi, result,
     load_sem, core_send, core_recv, one_send, one_recv, two_send, two_recv,
     hz_send, hz_recv, hy_send, hy_recv, out_send, out_recv,
@@ -192,7 +192,7 @@
 
     def ahead(i):
         k = i % 4
-        return jnp.where(k < 2, 2 * k + 1, 6 - 2 * k)
+        return (jnp.where(k < 2, 2 * k + 1, 6 - 2 * k) + 2 * core) % 4
 
     def piece(i):
         return (py + ahead(i)) % 4, i // 4
@@ -387,76 +387,92 @@
 
     lax.fori_loop(0, 4, arrive_body, 0)
 
-    lane = lax.broadcasted_iota(jnp.int32, (8, NX), 1)
-    x_mask = jnp.where(lane == NX - 1, 0.0, 1.0).astype(F32)
+    lane = lax.broadcasted_iota(jnp.int32, (8, 128), 1)
     y_mask = {
         1: jnp.where(jnp.logical_and(sub == 7, yb == 15), 0.0, 1.0).astype(F32),
         2: jnp.where(jnp.logical_and(sub == 7, yb == 0), 0.0, 1.0).astype(F32),
     }
     limit = threshold * threshold
 
+    def next_x(f):
+        parts = [f[:, k : k + 128] for k in range(0, f.shape[1], 128)]
+        turned = [pltpu.roll(p, 127, 1) for p in parts]
+        later = turned[1:] + parts[-1:]
+        return jnp.concatenate(
+            [jnp.where(lane == 127, b, a) for a, b in zip(turned, later)], axis=1
+        )
+
+    def last_x(p):
+        parts = [p[:, k : k + 128] for k in range(0, p.shape[1], 128)]
+        turned = [pltpu.roll(q, 1, 1) for q in parts]
+        earlier = [jnp.zeros_like(parts[0])] + turned[:-1]
+        return jnp.concatenate(
+            [jnp.where(lane == 0, b, a) for a, b in zip(turned, earlier)], axis=1
+        )
+
     def sweep(turn, first, last):
         src = (base, field_one, field_two)[turn]
         target = (field_one, field_two, result)[turn]
         dual = (dual_zero, dual_one, None)[turn]
+        div = (div_zero, div_one, None)[turn]
         dual_past = (None, dual_zero, dual_one)[turn]
+        div_past = (None, div_zero, div_one)[turn]
 
         def body(z, _):
             z_global = zb * 16 + z - HALO
-            z_mask = jnp.where(
-                jnp.logical_or(z_global == 127, z_global == -1), 0.0, 1.0
-            ).astype(F32)
+            edge = jnp.logical_or(z_global == 127, z_global == -1)
+            upper = z + jnp.where(edge, 0, 1)
             here = [[src[z, m, pl.ds(8 * t, 8), :] for m in range(3)] for t in range(3)]
             rolled = [[pltpu.roll(here[t][m], 7, 0) for m in range(3)] for t in range(3)]
 
-            def steps(t):
+            def duals(t):
                 rows = pl.ds(8 * t, 8)
-                values, old, squares = [], [], None
+                values, squares = [], None
                 for m in range(3):
                     f = here[t][m]
-                    along_z = (src[z + 1, m, rows, :] - f) * z_mask
+                    along_z = src[upper, m, rows, :] - f
                     along_y = jnp.where(sub == 7, rolled[(t + 1) % 3][m], rolled[t][m]) - f
                     if t:
                         along_y = along_y * y_mask[t]
-                    along_x = (pltpu.roll(f, NX - 1, 1) - f) * x_mask
+                    along_x = next_x(f) - f
                     triple = [along_z, along_y, along_x]
                     if turn:
-                        past = [dual_past[z, 3 * m + d, rows, :] for d in range(3)]
-                        triple = [a + b for a, b in zip(triple, past)]
-                        old.append(past)
+                        triple = [
+                            triple[d] + dual_past[z, 3 * m + d, rows, :] for d in range(3)
+                        ]
                     values.append(triple)
                     for v in triple:
                         squares = v * v if squares is None else squares + v * v
                 scale = threshold * lax.rsqrt(jnp.maximum(squares, limit))
-                twice = scale + scale
-                moved = []
-                for m in range(3):
-                    if turn < 2:
+                fresh = [[v * scale for v in triple] for triple in values]
+                if turn < 2:
+                    for m in range(3):
                         for d in range(3):
-                            dual[z, 3 * m + d, rows, :] = values[m][d] * scale
-                    triple = [v * twice for v in values[m]]
-                    if turn:
-                        triple = [a - b for a, b in zip(triple, old[m])]
-                    moved.append(triple)
-                return moved
-
-            def inner(t, moved):
+                            dual[z, 3 * m + d, rows, :] = fresh[m][d]
+                return fresh
+
+            def inner(t, fresh):
                 rows = pl.ds(8 * t, 8)
                 partial, turned = [], []
                 for m in range(3):
-                    step_z, step_y, step_x = moved[m]
-                    total = step_z - carry[turn, m, rows, :]
-                    carry[turn, m, rows, :] = step_z
-                    total = total + (step_x - pltpu.roll(step_x, 1, 1)) + step_y
-                    partial.append(total + 12.0 * here[t][m])
-                    turned.append(pltpu.roll(step_y, 1, 0))
+                    part_z, part_y, part_x = fresh[m]
+                    total = part_z - carry[turn, m, rows, :]
+                    carry[turn, m, rows, :] = part_z
+                    partial.append(total + (part_x - last_x(part_x)) + part_y)
+                    turned.append(pltpu.roll(part_y, 1, 0))
                 return partial, turned
 
             def finish(t, partial, own, earlier):
                 rows = pl.ds(8 * t, 8)
-                total = [
-                    partial[m] - jnp.where(sub == 0, earlier[m], own[m]) for m in range(3)
-                ]
+                total = []
+                for m in range(3):
+                    fresh_div = partial[m] - jnp.where(sub == 0, earlier[m], own[m])
+                    if turn < 2:
+                        div[z, m, rows, :] = fresh_div
+                    step_div = fresh_div + fresh_div
+                    if turn:
+                        step_div = step_div - div_past[z, m, rows, :]
+                    total.append(step_div + 12.0 * here[t][m])
                 for m in range(3):
                     value = (
                         base[z, m, rows, :]
@@ -466,14 +482,14 @@
                     )
                     target[z - 2 if turn == 2 else z, m, rows, :] = value
 
-            moved = steps(2)
+            fresh = duals(2)
             if turn < 2:
-                partial_two, turned_two = inner(2, moved)
+                partial_two, turned_two = inner(2, fresh)
             else:
-                turned_two = [pltpu.roll(moved[m][1], 1, 0) for m in range(3)]
-            partial, turned_zero = inner(0, steps(0))
+                turned_two = [pltpu.roll(fresh[m][1], 1, 0) for m in range(3)]
+            partial, turned_zero = inner(0, duals(0))
             finish(0, partial, turned_zero, turned_two)
-            partial, turned_one = inner(1, steps(1))
+            partial, turned_one = inner(1, duals(1))
             finish(1, partial, turned_one, turned_zero)
             if turn < 2:
                 finish(2, partial_two, turned_two, turned_one)
@@ -508,15 +524,29 @@
         def _():
             send(layer).start()
 
-    spread = py + 4 * (xl + 2 * pz0)
+
+    def layer_at(i):
+        a, b = i % 4, i // 4
+        low = (py + jnp.where(a < 2, 2 * a + 1, 6 - 2 * a) + 2 * core) % 4
+        bit = xl ^ 1 ^ core ^ (b % 2)
+        return low + 4 * bit + 8 * ((b // 2) ^ (a // 2) ^ pz1)
 
     def send_inner(i, _):
-        send_layer(3 + (i + spread) % 10)
+        layer = layer_at(i)
+
+        @pl.when(jnp.logical_and(layer >= 3, layer <= 12))
+        def _():
+            send_layer(layer)
+
         return 0
 
     def send_outer(i, _):
-        k = (i + spread) % 6
-        send_layer(jnp.where(k < 3, k, k + 10))
+        layer = layer_at(i)
+
+        @pl.when(jnp.logical_or(layer < 3, layer > 12))
+        def _():
+            send_layer(layer)
+
         return 0
 
     sweep(0, 3, 17)
@@ -542,7 +572,7 @@
 
     sweep(1, 4, 16)
     sweep(2, 5, 15)
-    lax.fori_loop(0, 10, send_inner, 0)
+    lax.fori_loop(0, 16, send_inner, 0)
     arrive_y(4)
     for at in range(8, 11):
         unpack_pair(at, True)
@@ -552,7 +582,7 @@
     sweep(1, 1, 4)
     sweep(2, 16, 18)
     sweep(2, 2, 5)
-    lax.fori_loop(0, 6, send_outer, 0)
+    lax.fori_loop(0, 16, send_outer, 0)
 
     def drain_swap(q, _):
         swap(q).wait_send()
@@ -616,6 +646,8 @@
             pltpu.VMEM((LAYERS, 3, 24, NX), F32),
             pltpu.VMEM((LAYERS, 9, 24, NX), F32),
             pltpu.VMEM((LAYERS, 9, 24, NX), F32),
+            pltpu.VMEM((LAYERS, 3, 24, NX), F32),
+            pltpu.VMEM((LAYERS, 3, 24, NX), F32),
             pltpu.VMEM((3, 3, 24, NX), F32),
             pltpu.VMEM((11, 3, 8, NX), F32),
             pltpu.VMEM((11, 3, 8, NX), F32),

time: 106 us -> 101 us (0.953)
  Pallas kernels: 102 us -> 97.6 us
    pallas_call x1, Pallas kernels: 102 us -> 97.6 us  [on_device(): pl.pallas_call(kernel, out_shape=jax.ShapeDtypeStruct((3, 256, NX), F32),...]
where the time goes in v3:
time: 101 us
  Pallas kernels  97.6 us (97%)
  local copies, waits for them, and re-layouts  1.82 us (2%)
  between operations  1.31 us (1%)
    pallas_call x1, Pallas kernels, on_device(): pl.pallas_call(kernel, out_shape=jax.ShapeDtypeStruct((3, 256, NX), F32),...  97.6 us

profile of v3, /device:TPU:9, one launch (start us, length us, event | category | flops | bytes accessed | tf_op | source)
XLA Modules:
  0.0 100.8 jit_solution(7115097903980203681)
XLA Ops:
  1.3 0.0 copy-start
  1.3 0.7 copy-done
  2.0 97.6 %shard_map.46 = f32[3,256,512]{2,1,0:T(8,128)S(1)} custom-call(f32[2,4,8,2,16,512]{5,4,3,2,1,0:T(8,128)} %bitcast.7, f32[3,8]{1,0:T(4,128)S(1)} %bitcast.6, f32[1]{0:T(128)S(6)} %copy.7.penalty, f32[1]{0:T(128)S(6)} %copy.8.tv_weight), custom_call_target="tpu_custom_call" | custom-call | flops 60000000 | bytes 8000000 | tf_op jit(solution)/shard_map/pallas_call | solution.py:633
  99.6 1.1 %copy.9 = f32[3,1,256,512]{3,2,1,0:T(8,128)} copy(f32[3,1,256,512]{3,2,1,0:T(8,128)S(1)} %bitcast.5) | data formatting | bytes 3145728
Async XLA Ops:
  1.3 0.7 copy-start

commit v4 on v3

--- a/solution.py
+++ b/solution.py
@@ -410,7 +410,7 @@
             [jnp.where(lane == 0, b, a) for a, b in zip(turned, earlier)], axis=1
         )
 
-    def sweep(turn, first, last):
+    def sweep(turn, first, last, chain):
         src = (base, field_one, field_two)[turn]
         target = (field_one, field_two, result)[turn]
         dual = (dual_zero, dual_one, None)[turn]
@@ -456,8 +456,8 @@
                 partial, turned = [], []
                 for m in range(3):
                     part_z, part_y, part_x = fresh[m]
-                    total = part_z - carry[turn, m, rows, :]
-                    carry[turn, m, rows, :] = part_z
+                    total = part_z - carry[chain, turn, m, rows, :]
+                    carry[chain, turn, m, rows, :] = part_z
                     partial.append(total + (part_x - last_x(part_x)) + part_y)
                     turned.append(pltpu.roll(part_y, 1, 0))
                 return partial, turned
@@ -531,25 +531,22 @@
         bit = xl ^ 1 ^ core ^ (b % 2)
         return low + 4 * bit + 8 * ((b // 2) ^ (a // 2) ^ pz1)
 
-    def send_inner(i, _):
-        layer = layer_at(i)
-
-        @pl.when(jnp.logical_and(layer >= 3, layer <= 12))
-        def _():
-            send_layer(layer)
-
-        return 0
-
-    def send_outer(i, _):
-        layer = layer_at(i)
-
-        @pl.when(jnp.logical_or(layer < 3, layer > 12))
-        def _():
-            send_layer(layer)
-
-        return 0
-
-    sweep(0, 3, 17)
+    def send_layers(first, last):
+        def body(i, _):
+            layer = layer_at(i)
+
+            @pl.when(jnp.logical_and(layer >= first, layer <= last))
+            def _():
+                send_layer(layer)
+
+            return 0
+
+        lax.fori_loop(0, 16, body, 0)
+
+    def either(zero, one):
+        return jnp.where(core == 0, zero, one)
+
+    sweep(0, either(3, 8), either(12, 17), 0)
     for n in range(3):
         @pl.when(has_above)
         def _():
@@ -570,19 +567,26 @@
     def _():
         halo_y(1, 4).start()
 
-    sweep(1, 4, 16)
-    sweep(2, 5, 15)
-    lax.fori_loop(0, 16, send_inner, 0)
+    sweep(1, either(4, 9), either(11, 16), 0)
+    sweep(2, either(5, 10), either(10, 15), 0)
+    send_layers(either(3, 8), either(7, 12))
+    sweep(0, either(13, 3), either(17, 8), core)
+    sweep(1, either(12, 4), either(16, 9), core)
+    sweep(2, either(11, 5), either(15, 10), core)
+    send_layers(either(8, 3), either(12, 7))
     arrive_y(4)
     for at in range(8, 11):
         unpack_pair(at, True)
-    sweep(0, 18, 20)
-    sweep(0, 0, 3)
-    sweep(1, 17, 19)
-    sweep(1, 1, 4)
-    sweep(2, 16, 18)
-    sweep(2, 2, 5)
-    lax.fori_loop(0, 16, send_outer, 0)
+    for half in range(2):
+        upper = core == half
+        for turn in range(3):
+            sweep(
+                turn,
+                jnp.where(upper, 18 - turn, turn),
+                jnp.where(upper, 20 - turn, 3 + turn),
+                jnp.where(upper, 0, 1),
+            )
+        send_layers(jnp.where(upper, 13, 0), jnp.where(upper, 15, 2))
 
     def drain_swap(q, _):
         swap(q).wait_send()
@@ -648,7 +652,7 @@
             pltpu.VMEM((LAYERS, 9, 24, NX), F32),
             pltpu.VMEM((LAYERS, 3, 24, NX), F32),
             pltpu.VMEM((LAYERS, 3, 24, NX), F32),
-            pltpu.VMEM((3, 3, 24, NX), F32),
+            pltpu.VMEM((2, 3, 3, 24, NX), F32),
             pltpu.VMEM((11, 3, 8, NX), F32),
             pltpu.VMEM((11, 3, 8, NX), F32),
             pltpu.VMEM((11, 3, 8, NX), F32),

time: 101 us -> 99.9 us (0.989); the launches traced: 101 us -> 98.4 us
  Pallas kernels: 97.6 us -> 95.2 us
    pallas_call x1, Pallas kernels: 97.6 us -> 95.2 us  [on_device(): pl.pallas_call(kernel, out_shape=jax.ShapeDtypeStruct((3, 256, NX), F32),...]
where the time goes in v4:
time: 99.9 us; the launch traced here: 98.4 us
  Pallas kernels  95.2 us (95%)
  local copies, waits for them, and re-layouts  1.82 us (2%)
  between operations  1.31 us (1%)
    pallas_call x1, Pallas kernels, on_device(): pl.pallas_call(kernel, out_shape=jax.ShapeDtypeStruct((3, 256, NX), F32),...  95.2 us

profile of v4, /device:TPU:9, one launch (start us, length us, event | category | flops | bytes accessed | tf_op | source)
XLA Modules:
  0.0 98.4 jit_solution(4744395941817570525)
XLA Ops:
  1.3 0.0 copy-start
  1.3 0.7 copy-done
  2.0 95.2 %shard_map.46 = f32[3,256,512]{2,1,0:T(8,128)S(1)} custom-call(f32[2,4,8,2,16,512]{5,4,3,2,1,0:T(8,128)} %bitcast.7, f32[3,8]{1,0:T(4,128)S(1)} %bitcast.6, f32[1]{0:T(128)S(6)} %copy.7.penalty, f32[1]{0:T(128)S(6)} %copy.8.tv_weight), custom_call_target="tpu_custom_call" | custom-call | flops 60000000 | bytes 8000000 | tf_op jit(solution)/shard_map/pallas_call | solution.py:637
  97.2 1.1 %copy.9 = f32[3,1,256,512]{3,2,1,0:T(8,128)} copy(f32[3,1,256,512]{3,2,1,0:T(8,128)S(1)} %bitcast.5) | data formatting | bytes 3145728
Async XLA Ops:
  1.3 0.7 copy-start

commit v5 on v4

--- a/solution.py
+++ b/solution.py
@@ -547,6 +547,7 @@
         return jnp.where(core == 0, zero, one)
 
     sweep(0, either(3, 8), either(12, 17), 0)
+    sweep(1, either(4, 9), either(11, 16), 0)
     for n in range(3):
         @pl.when(has_above)
         def _():
@@ -567,7 +568,6 @@
     def _():
         halo_y(1, 4).start()
 
-    sweep(1, either(4, 9), either(11, 16), 0)
     sweep(2, either(5, 10), either(10, 15), 0)
     send_layers(either(3, 8), either(7, 12))
     sweep(0, either(13, 3), either(17, 8), core)

time: 99.9 us -> 98.2 us (0.983); the launches traced: 98.4 us -> 98.1 us
  no operation moved by 1% of the time
where the time goes in v5:
time: 98.2 us; the launch traced here: 98.1 us
  Pallas kernels  94.9 us (97%)
  local copies, waits for them, and re-layouts  1.82 us (2%)
  between operations  1.31 us (1%)
    pallas_call x1, Pallas kernels, on_device(): pl.pallas_call(kernel, out_shape=jax.ShapeDtypeStruct((3, 256, NX), F32),...  94.9 us

profile of v5, /device:TPU:9, one launch (start us, length us, event | category | flops | bytes accessed | tf_op | source)
XLA Modules:
  0.0 98.1 jit_solution(12574182645948356669)
XLA Ops:
  1.3 0.0 copy-start
  1.3 0.7 copy-done
  2.0 94.9 %shard_map.46 = f32[3,256,512]{2,1,0:T(8,128)S(1)} custom-call(f32[2,4,8,2,16,512]{5,4,3,2,1,0:T(8,128)} %bitcast.7, f32[3,8]{1,0:T(4,128)S(1)} %bitcast.6, f32[1]{0:T(128)S(6)} %copy.7.penalty, f32[1]{0:T(128)S(6)} %copy.8.tv_weight), custom_call_target="tpu_custom_call" | custom-call | flops 60000000 | bytes 8000000 | tf_op jit(solution)/shard_map/pallas_call | solution.py:637
  96.9 1.1 %copy.9 = f32[3,1,256,512]{3,2,1,0:T(8,128)} copy(f32[3,1,256,512]{3,2,1,0:T(8,128)S(1)} %bitcast.5) | data formatting | bytes 3145728
Async XLA Ops:
  1.3 0.7 copy-start
